TPU v7x, 256 devices: a whole 4x4x8 slice. The times are simulated.
256 devices in a mesh: lat: 4 (over y_hi, core), lon: 64 (over x, y_lo, z).
Axes of the slice: x: 4, y: 4 (y_hi: 2, y_lo: 2; y = y_hi * 2 + y_lo), z: 8, core: 2. Of those that a mesh axis runs over, the one named last changes fastest.
Arguments:
- field: bfloat16 [64, 4096, 256], P('lat', 'lon'), may hold values from -6 to 6
- filters: bfloat16 [64, 4, 9, 264], P('lat'), may hold values from -0.1875 to 0.1875
- sector_width: int32 [8], P('lat'), may hold values from 1 to 2, as said below
- block_offset: int32 [8, 4], P('lat'), may hold values from -8 to 7, as said below
- mixing: bfloat16 [9, 32, 256], replicated, may hold values from -0.375 to 0.375
Outputs:
- output: bfloat16 [64, 4096, 256], P('lat', 'lon')
Inputs may be any that keep to these rules, and one draw needn't show every extreme that they name: `sector_width`: the last row group has width 2, some row group has width 1. `block_offset`: in units of 8 longitudes; the last row group holds both ends of the range.
All inputs are finite; a program needn't handle non-finite values.
Results may differ from a plain program's by a relative error of at most 0.0049.
Values may be sent and summed in bfloat16 or wider, within the bound.
No kernel may reach another device: no remote copies, remote signals or barrier semaphores. Data moves between devices by JAX's collectives and lax.ppermute only.
A program may use at most 128 MiB of HBM per device.

v0:
```python
import functools

import jax
import jax.numpy as jnp
from jax import lax
from jax.experimental import pallas as pl
from jax.experimental.pallas import tpu as pltpu
from jax.sharding import PartitionSpec as P

K = 9
G = 8
R = 16
RG = 8
NB = 4
BW = 8
SMAX = 2
J = 2
T = BW + J - 1
SECTORS = 2 * SMAX + 1
PADDED = 384
VMEM = pl.BlockSpec(memory_space=pltpu.VMEM)
SMEM = pl.BlockSpec(memory_space=pltpu.SMEM)
ANY = pl.BlockSpec(memory_space=pl.ANY)


def lat_swap(value, flip):
    return lax.ppermute(value, "lat", [(lat, lat ^ flip) for lat in range(4)])


def pair_swap(value, odd):
    count = lax.axis_size("lon")
    pairs = [(s, (((s + odd) ^ 1) - odd) % count) for s in range(count)]
    return lax.ppermute(value, "lon", pairs)


def halo(value):
    near, back = pair_swap(value, 0), pair_swap(value, 1)
    return near, back


def beyond(near, back):
    return pair_swap(back, 0), pair_swap(near, 1)


def prep_kernel(place_ref, filt_ref, far_ref, near_ref, spread_ref, pick_ref):
    upper = place_ref[0]
    far = place_ref[1]
    deep, wide = NB * 128, T * NB * R

    row = lax.broadcasted_iota(jnp.int32, (deep, wide), 0)
    col = lax.broadcasted_iota(jnp.int32, (1, wide), 1)
    for j in range(J):
        t = (col >> 6) - j
        target = ((col >> 4) & 3) * 128 + (col & 15) * BW + t
        hit = jnp.where((row == target) & (t >= 0) & (t < BW), 1.0, 0.0)
        pick_ref[j] = hit.astype(jnp.bfloat16)

    for which in range(2):
        half = jnp.where(far == 1, which, 1 - which)
        base = 1 - upper if which == 0 else upper
        for g in range(2):
            for p in range(RG):
                i = g * RG + p
                for b in range(NB):
                    x = filt_ref[half, i, b].astype(jnp.float32)
                    if i:
                        x = pltpu.roll(x, BW * i, 1)
                    for n in range(PADDED // 128):
                        spread_ref[n, b, pl.ds(p, K, stride=RG), :] = x[:, n * 128 : (n + 1) * 128]

            def lay(band, n):
                left = jnp.concatenate([spread_ref[band, b] for b in range(NB)], axis=1)
                left = left.astype(jnp.bfloat16)
                sides = [
                    jnp.dot(left, pick_ref[j], preferred_element_type=jnp.float32)
                    for j in range(J)
                ]
                for k in range(K):
                    both = jnp.concatenate([s[k * RG : (k + 1) * RG] for s in sides], axis=0)
                    columns = slice(n * wide, (n + 1) * wide)
                    ref = (far_ref, near_ref)[which]
                    ref[g, k * 16 : (k + 1) * 16, columns] = both.astype(jnp.bfloat16)

            lay(base, 0)
            lay(base + 1, 1)
            if which:
                lay(2 * (1 - upper), 2)


def left_sides(place, filters):
    wide = T * NB * R
    return pl.pallas_call(
        prep_kernel,
        out_shape=[
            jax.ShapeDtypeStruct((2, K * J * RG, sets * wide), jnp.bfloat16) for sets in (2, 3)
        ],
        in_specs=[SMEM, VMEM],
        out_specs=[VMEM] * 2,
        scratch_shapes=[
            pltpu.VMEM((PADDED // 128, NB, K * RG, 128), jnp.float32),
            pltpu.VMEM((J, NB * 128, wide), jnp.bfloat16),
        ],
        compiler_params=pltpu.CompilerParams(vmem_limit_bytes=16 << 20),
        cost_estimate=pl.CostEstimate(flops=1, bytes_accessed=1, transcendentals=0),
    )(place, filters)


def fetch(place_ref, pieces, ext, sems):
    lon = pieces[0].shape[0]
    odd = place_ref[2]
    sectors = (SMAX, 3 - 2 * odd, 1 + 2 * odd, 4 - 4 * odd, 4 * odd)
    copies = []
    for n, piece in enumerate(pieces):
        target = ext.at[pl.ds(sectors[n] * lon, lon)]
        copies.append(pltpu.make_async_copy(piece, target, sems.at[n]))
    return copies


def product(left, exts, shifts, jb, lon):
    columns = []
    for side in range(2):
        at = SMAX * lon + jb * J + side * (lon // 2)
        starts = [at + shift for shift in shifts]
        rows = []
        for ext in exts:
            for first in range(0, ext.shape[1], R):
                for t in range(T):
                    for start in starts:
                        rows.append(ext[start + t, first : first + R, :])
        columns.append(jnp.concatenate(rows, axis=0))
    right = jnp.concatenate(columns, axis=1)
    return jnp.dot(left, right, preferred_element_type=jnp.float32)


def keep(resp_ref, resp, jb):
    resp = resp.astype(jnp.bfloat16)
    width = resp.shape[1]
    rows = pl.ds(pl.multiple_of(jb * 16, 16), 16)
    for k in range(K):
        resp_ref[rows, k * width : (k + 1) * width] = resp[k * 16 : (k + 1) * 16]


def mix_rows(resp_ref, mix_ref, mixed_ref, out_ref, g):
    mixed = jnp.dot(resp_ref[...], mix_ref[...], preferred_element_type=jnp.float32)
    chans = mixed.shape[1] // 2
    half = mixed.shape[0] // RG
    for side in range(2):
        mixed_ref[side] = mixed[:, side * chans : (side + 1) * chans]
        for p in range(RG):
            rows = mixed_ref[side, pl.ds(p, half, stride=RG), :]
            out_ref[g, p, side * half : (side + 1) * half, :] = rows.astype(jnp.bfloat16)


def conv_kernel(early, whiches, counts, place_ref, shift_ref, *refs):
    sets = []
    for count in counts:
        sets.append(refs[:count])
        refs = refs[count:]
    some = len(whiches)
    left_refs, mix_ref, refs = refs[:some], refs[some], refs[some + 1 :]
    if not early:
        done_refs, refs = refs[:some], refs[some:]
    out_refs, refs = refs[:some], refs[some:]
    exts, (resp_ref, mixed_ref, sems) = refs[: len(sets)], refs[len(sets) :]
    lon = sets[0][0].shape[0]
    copies = []
    for i, pieces in enumerate(sets):
        copies += fetch(place_ref, pieces, exts[i], sems.at[i])
    for copy in copies:
        copy.start()
    for copy in copies:
        copy.wait()
    for n, which in enumerate(whiches):
        left_ref, out_ref = left_refs[n], out_refs[n]

        def group(g, carry):
            shifts = [shift_ref[2 * which + g, b] for b in range(NB)]
            local = True
            for shift in shifts:
                local = local & (shift >= -lon) & (shift <= lon - BW)

            @pl.when(local if early else jnp.logical_not(local))
            def _():
                def step(jb, carry):
                    keep(resp_ref, product(left_ref[g], exts[: 1 + which], shifts, jb, lon), jb)
                    return carry

                lax.fori_loop(0, lon // 2 // J, step, 0, unroll=True)
                mix_rows(resp_ref, mix_ref, mixed_ref, out_ref, g)

            if not early:

                @pl.when(local)
                def _():
                    out_ref[g] = done_refs[n][g]

            return carry

        lax.fori_loop(0, 2, group, 0)


def conv(whiches, place, shifts, sets, lefts, mix, done=()):
    lon, _, chans = sets[0][0].shape
    half = lon // 2
    counts = [len(pieces) for pieces in sets]
    arrays = [*lefts, mix, *done]
    return pl.pallas_call(
        functools.partial(conv_kernel, not done, whiches, counts),
        out_shape=[jax.ShapeDtypeStruct((2, RG, lon, chans), jnp.bfloat16)] * len(whiches),
        in_specs=[SMEM, SMEM] + [ANY] * sum(counts) + [VMEM] * len(arrays),
        out_specs=[VMEM] * len(whiches),
        scratch_shapes=[
            pltpu.VMEM((SECTORS * lon, pieces[0].shape[1], chans), jnp.bfloat16) for pieces in sets
        ]
        + [
            pltpu.VMEM((half * RG, K * 2 * chans), jnp.bfloat16),
            pltpu.VMEM((2, half * RG, chans), jnp.float32),
            pltpu.SemaphoreType.DMA((len(sets), SECTORS)),
        ],
        compiler_params=pltpu.CompilerParams(vmem_limit_bytes=24 << 20),
        cost_estimate=pl.CostEstimate(flops=1, bytes_accessed=1, transcendentals=0),
    )(place, shifts, *[x for pieces in sets for x in pieces], *arrays)


def together(*values):
    return lax.optimization_barrier(values)


def on_device(field, filters, sector_width, block_offset, mixing):
    rows, lon, chans = field.shape
    half = chans // 2
    lat = lax.axis_index("lat")
    upper, core = lat // 2, lat % 2
    first = core == 0
    far = core == upper
    place = jnp.stack([upper, far.astype(jnp.int32), lax.axis_index("lon") % 2]).astype(jnp.int32)

    turned = field.transpose(1, 0, 2)
    low, high = turned[:, :, :half], turned[:, :, half:]
    mine, theirs = together(jnp.where(first, low, high), jnp.where(first, high, low))
    got = lat_swap(theirs, 1)
    filters, block_offset, mixing, mine = together(filters, block_offset, mixing, mine)
    shifts = BW * block_offset * sector_width[:, None]
    other_shifts = lat_swap(shifts, 1)
    other_filters = lat_swap(filters, 1)

    got, mine, filters, mixing = together(got, mine, filters, mixing)
    top, bottom = jnp.where(first, mine, got), jnp.where(first, got, mine)
    own = jnp.concatenate([top, bottom], axis=1)
    edge = lat_swap(jnp.where(upper == 0, bottom, top), 2)
    own_near = pair_swap(own, 0)
    own_late, edge, filters, other_filters, mixing = together(
        own, edge, filters, other_filters, mixing
    )
    own_back = pair_swap(own_late, 1)
    edge_near, edge_back = halo(edge)

    both = jnp.stack([filters, other_filters])
    both = jnp.pad(both, ((0, 0),) * 4 + ((0, PADDED - both.shape[-1]),))
    far_left, near_left = left_sides(place, both)
    far_shifts = jnp.where(far, shifts, other_shifts)
    near_shifts = jnp.where(far, other_shifts, shifts)
    all_shifts = jnp.concatenate([far_shifts, near_shifts], axis=0)

    group_chans = chans // G
    side = lax.dynamic_slice_in_dim(mixing, core * half, half, axis=2)
    tiled = jnp.tile(side, (1, chans // group_chans, 2))
    row_at = lax.broadcasted_iota(jnp.int32, (chans, chans), 0) // group_chans
    col_at = lax.broadcasted_iota(jnp.int32, (chans, chans), 1) // group_chans
    mix = jnp.where((row_at == col_at)[None], tiled, jnp.zeros_like(tiled))
    mix = mix.reshape(K * chans, chans)

    far_left, near_left, mix, own_near, own_back = together(
        far_left, near_left, mix, own_near, own_back
    )
    own_far_near, own_far_back = beyond(own_near, own_back)
    own_set, edge_set = [own, own_near, own_back], [edge, edge_near, edge_back]
    (far_done,) = conv([0], place, all_shifts, [own_set], [far_left], mix)
    edge_near, edge_back, far_done = together(edge_near, edge_back, far_done)
    edge_set = [edge, edge_near, edge_back]
    edge_far_near, edge_far_back = beyond(edge_near, edge_back)
    (near_done,) = conv([1], place, all_shifts, [own_set, edge_set], [near_left], mix)
    own_far_near, own_far_back, near_done = together(own_far_near, own_far_back, near_done)
    own_set = own_set + [own_far_near, own_far_back]
    (far_out,) = conv([0], place, all_shifts, [own_set], [far_left], mix, [far_done])
    edge_far_near, edge_far_back, far_out = together(edge_far_near, edge_far_back, far_out)
    edge_set = edge_set + [edge_far_near, edge_far_back]
    sets = [own_set, edge_set]
    (near_out,) = conv([1], place, all_shifts, sets, [near_left], mix, [near_done])

    far_out, near_out = (x.reshape(rows, lon, half) for x in (far_out, near_out))
    kept = jnp.where(far, far_out, near_out)
    other = lat_swap(jnp.where(far, near_out, far_out), 1)
    return jnp.concatenate([jnp.where(first, kept, other), jnp.where(first, other, kept)], axis=2)


def solution(mesh):
    return jax.shard_map(
        on_device,
        mesh=mesh,
        in_specs=(P("lat", "lon", None), P("lat", None, None, None), P("lat"), P("lat", None), P()),
        out_specs=P("lat", "lon", None),
        check_vma=False,
    )
```

profile of v0, /device:TPU:17, one launch (start us, length us, event | category | flops | bytes accessed | tf_op | source)
XLA Modules:
  0.0 64.7 jit_solution(10906233123717881210)
XLA Ops:
  0.0 1.4 %copy.18 = bf16[16,64,256]{2,0,1:T(8,128)(2,1)S(1)} copy(bf16[16,64,256]{2,1,0:T(8,128)(2,1)} %param.5) | data formatting | bytes 1048576 | tf_op args[0]
  1.5 0.8 %collective-permute-start = (bf16[64,16,128]{2,1,0:T(8,128)(2,1)S(1)}, bf16[64,16,128]{2,1,0:T(8,128)(2,1)S(1)}, u32[]{:S(2)}, u32[]{:S(2)}) collective-permute-start(bf16[64,16,128]{2,1,0:T(8,128)(2,1)S(1)} %get-tuple-element.36), channel_id=1, source_target_pairs={{0,64},{64,0},{128,192},{192,128},{1,65},{65,1},{129,193},{193,129... | collective-permute-start | bytes 786440 | tf_op jit(solution)/shard_map/ppermute | solution.py:27
  2.5 0.5 collective-permute-start.5
  3.0 0.4 collective-permute-done
  3.5 1.9 %collective-permute-start.1 = (bf16[64,16,128]{2,1,0:T(8,128)(2,1)S(1)}, bf16[64,16,128]{2,1,0:T(8,128)(2,1)S(1)}, u32[]{:S(2)}, u32[]{:S(2)}) collective-permute-start(bf16[64,16,128]{2,1,0:T(8,128)(2,1)S(1)} %get-tuple-element.67), channel_id=1, source_target_pairs={{0,128},{64,192},{128,0},{192,64},{1,129},{65,193},{129,1},{193,65... | collective-permute-start | bytes 786440 | tf_op jit(solution)/shard_map/ppermute | solution.py:27
  5.3 0.2 select_compare_fusion
  5.8 6.8 %collective-permute-done.1.refs_3_.refs_5_ = bf16[64,16,128]{2,1,0:T(8,128)(2,1)S(1)} collective-permute-done((bf16[64,16,128]{2,1,0:T(8,128)(2,1)S(1)}, bf16[64,16,128]{2,1,0:T(8,128)(2,1)S(1)}, u32[]{:S(2)}, u32[]{:S(2)}) %collective-permute-start.1) | collective-permute-done | bytes 262176 | tf_op jit(solution)/shard_map/ppermute | solution.py:27
  12.6 8.5 %collective-permute-start.7 = (bf16[64,32,128]{2,1,0:T(8,128)(2,1)S(1)}, bf16[64,32,128]{2,1,0:T(8,128)(2,1)S(1)}, u32[]{:S(2)}, u32[]{:S(2)}) collective-permute-start(bf16[64,32,128]{2,1,0:T(8,128)(2,1)S(1)} %pad_maximum_fusion.refs_0_), channel_id=1, source_target_pairs={{0,63},{1,2},{2,1},{3,4},{4,3},{5,6},{6,5},{7,8},{8,7},{9,10},{10,... | collective-permute-start | bytes 1572872 | tf_op jit(solution)/shard_map/ppermute | solution.py:33
  21.1 0.3 copy_bitcast_fusion
  21.4 0.4 fusion.2.filt_ref
  21.8 1.5 %collective-permute-start.4 = (bf16[64,16,128]{2,1,0:T(8,128)(2,1)S(1)}, bf16[64,16,128]{2,1,0:T(8,128)(2,1)S(1)}, u32[]{:S(2)}, u32[]{:S(2)}) collective-permute-start(bf16[64,16,128]{2,1,0:T(8,128)(2,1)S(1)} %collective-permute-done.1.refs_3_.refs_5_), channel_id=1, source_target_pairs={{0,63},{1,2},{2,1},{3,4},{4,3},{5,6},{6,5},{7,8},{8,7},{9,10},{10,... | collective-permute-start | bytes 786440 | tf_op jit(solution)/shard_map/ppermute | solution.py:33
  23.3 3.9 %shard_map.55 = (bf16[2,144,1152]{2,1,0:T(8,128)(2,1)S(1)}, bf16[2,144,1728]{2,1,0:T(8,128)(2,1)S(1)}) custom-call(s32[3]{0:T(128)S(1)} %pad_add_fusion.1.place_ref, bf16[2,16,4,9,384]{4,3,2,1,0:T(8,128)(2,1)S(1)} %fusion.2.filt_ref), custom_call_target="tpu_custom_call" | custom-call | flops 1 | bytes 1 | tf_op jit(solution)/shard_map/pallas_call | solution.py:92
  27.3 1.1 %tile.4 = bf16[9,8,32,2,128]{4,3,2,1,0:T(2,128)(2,1)S(1)} broadcast(bf16[9,32,128]{2,1,0:T(8,128)(2,1)S(1)} %constant_dynamic-slice_fusion), dimensions={0,2,4} | broadcast | bytes 1253376 | tf_op jit(solution)/shard_map/tile | solution.py:267
  28.4 0.2 bitcast_select_fusion.refs_4_.refs_7_.refs_6_.refs_11_
  28.6 3.5 %collective-permute-done.7.refs_2_ = bf16[64,32,128]{2,1,0:T(8,128)(2,1)S(1)} collective-permute-done((bf16[64,32,128]{2,1,0:T(8,128)(2,1)S(1)}, bf16[64,32,128]{2,1,0:T(8,128)(2,1)S(1)}, u32[]{:S(2)}, u32[]{:S(2)}) %collective-permute-start.7) | collective-permute-done | bytes 524320 | tf_op jit(solution)/shard_map/ppermute | solution.py:33
  32.1 5.4 %collective-permute-start.11 = (bf16[64,32,128]{2,1,0:T(8,128)(2,1)S(1)}, bf16[64,32,128]{2,1,0:T(8,128)(2,1)S(1)}, u32[]{:S(2)}, u32[]{:S(2)}) collective-permute-start(bf16[64,32,128]{2,1,0:T(8,128)(2,1)S(1)} %collective-permute-done.6.refs_1_), channel_id=1, source_target_pairs={{0,63},{1,2},{2,1},{3,4},{4,3},{5,6},{6,5},{7,8},{8,7},{9,10},{10,... | collective-permute-start | bytes 1572872 | tf_op jit(solution)/shard_map/ppermute | solution.py:33
  37.6 0.8 %shard_map.56.refs_7_ = bf16[2,8,64,128]{3,2,1,0:T(8,128)(2,1)S(1)} custom-call(s32[3]{0:T(128)S(1)} %pad_add_fusion.1.place_ref, s32[4,4]{1,0:T(4,128)S(1)} %pad_add_fusion.shift_ref, bf16[64,32,128]{2,1,0:T(8,128)(2,1)S(1)} %pad_maximum_fusion.refs_0_, bf16[64,32,128]{2,1,0:T(8,128)(2,1)S(1)} %collective-permute-done.6.refs_1_, ...), custom_call_target="tpu_custom_call" | custom-call | flops 1 | bytes 1 | tf_op jit(solution)/shard_map/pallas_call | solution.py:207
  38.5 4.6 %collective-permute-start.9 = (bf16[64,16,128]{2,1,0:T(8,128)(2,1)S(1)}, bf16[64,16,128]{2,1,0:T(8,128)(2,1)S(1)}, u32[]{:S(2)}, u32[]{:S(2)}) collective-permute-start(bf16[64,16,128]{2,1,0:T(8,128)(2,1)S(1)} %collective-permute-done.3.refs_4_.refs_6_), channel_id=1, source_target_pairs={{0,63},{1,2},{2,1},{3,4},{4,3},{5,6},{6,5},{7,8},{8,7},{9,10},{10,... | collective-permute-start | bytes 786440 | tf_op jit(solution)/shard_map/ppermute | solution.py:33
  43.1 3.9 %shard_map.57.refs_12_ = bf16[2,8,64,128]{3,2,1,0:T(8,128)(2,1)S(1)} custom-call(s32[3]{0:T(128)S(1)} %pad_add_fusion.1.place_ref, s32[4,4]{1,0:T(4,128)S(1)} %pad_add_fusion.shift_ref, bf16[64,32,128]{2,1,0:T(8,128)(2,1)S(1)} %pad_maximum_fusion.refs_0_, bf16[64,32,128]{2,1,0:T(8,128)(2,1)S(1)} %collective-permute-done.6.refs_1_, ...), custom_call_target="tpu_custom_call" | custom-call | flops 1 | bytes 1 | tf_op jit(solution)/shard_map/pallas_call | solution.py:207
  47.1 5.1 %shard_map.58 = bf16[2,8,64,128]{3,2,1,0:T(8,128)(2,1)S(1)} custom-call(s32[3]{0:T(128)S(1)} %pad_add_fusion.1.place_ref, s32[4,4]{1,0:T(4,128)S(1)} %pad_add_fusion.shift_ref, bf16[64,32,128]{2,1,0:T(8,128)(2,1)S(1)} %pad_maximum_fusion.refs_0_, bf16[64,32,128]{2,1,0:T(8,128)(2,1)S(1)} %collective-permute-done.6.refs_1_, ...), custom_call_target="tpu_custom_call" | custom-call | flops 1 | bytes 1 | tf_op jit(solution)/shard_map/pallas_call | solution.py:207
  52.3 3.8 %shard_map.59 = bf16[2,8,64,128]{3,2,1,0:T(8,128)(2,1)S(1)} custom-call(s32[3]{0:T(128)S(1)} %pad_add_fusion.1.place_ref, s32[4,4]{1,0:T(4,128)S(1)} %pad_add_fusion.shift_ref, bf16[64,32,128]{2,1,0:T(8,128)(2,1)S(1)} %pad_maximum_fusion.refs_0_, bf16[64,32,128]{2,1,0:T(8,128)(2,1)S(1)} %collective-permute-done.6.refs_1_, ...), custom_call_target="tpu_custom_call" | custom-call | flops 1 | bytes 1 | tf_op jit(solution)/shard_map/pallas_call | solution.py:207
  56.2 6.5 %collective-permute-start.12 = (bf16[16,64,128]{2,1,0:T(8,128)(2,1)S(1)}, bf16[16,64,128]{2,1,0:T(8,128)(2,1)S(1)}, u32[]{:S(2)}, u32[]{:S(2)}) collective-permute-start(bf16[16,64,128]{2,1,0:T(8,128)(2,1)S(1)} %bitcast.22), channel_id=1, source_target_pairs={{0,64},{64,0},{128,192},{192,128},{1,65},{65,1},{129,193},{193,129... | collective-permute-start | bytes 786440 | tf_op jit(solution)/shard_map/ppermute | solution.py:27
  62.6 1.2 %collective-permute-done.12 = bf16[16,64,128]{2,1,0:T(8,128)(2,1)S(1)} collective-permute-done((bf16[16,64,128]{2,1,0:T(8,128)(2,1)S(1)}, bf16[16,64,128]{2,1,0:T(8,128)(2,1)S(1)}, u32[]{:S(2)}, u32[]{:S(2)}) %collective-permute-start.12) | collective-permute-done | bytes 262176 | tf_op jit(solution)/shard_map/ppermute | solution.py:27
  63.8 0.9 %pad_maximum_fusion.1 = bf16[16,64,256]{2,1,0:T(8,128)(2,1)} fusion(bf16[16,64,128]{2,1,0:T(8,128)(2,1)S(1)} %get-tuple-element.71, bf16[16,64,128]{2,1,0:T(8,128)(2,1)S(1)} %get-tuple-element.70), kind=kLoop, calls=%fused_computation.8 | loop fusion | flops 1048576 | bytes 1048576 | tf_op jit(solution)/shard_map/concatenate | solution.py:294
  (36 shorter events, 1.1 us)
Async XLA Ops:
  0.0 27.2 %copy-start = (bf16[9,32,256]{2,1,0:T(8,128)(2,1)S(1)}, bf16[9,32,256]{2,1,0:T(8,128)(2,1)}, u32[]{:S(2)}) copy-start(bf16[9,32,256]{2,1,0:T(8,128)(2,1)} %param.9) | copy-start | bytes 442372
  0.0 2.2 %copy-start.1 = (bf16[16,4,9,264]{3,1,2,0:T(4,128)(2,1)S(1)}, bf16[16,4,9,264]{3,1,2,0:T(4,128)(2,1)}, u32[]{:S(2)}) copy-start(bf16[16,4,9,264]{3,1,2,0:T(4,128)(2,1)} %param.6) | copy-start | bytes 912388
  0.0 2.4 %copy-start.2 = (s32[2,4]{1,0:T(2,128)S(1)}, s32[2,4]{1,0:T(2,128)}, u32[]{:S(2)}) copy-start(s32[2,4]{1,0:T(2,128)} %param.8) | copy-start | bytes 100
  0.0 2.4 %copy-start.3 = (s32[2]{0:T(128)S(1)}, s32[2]{0:T(128)}, u32[]{:S(2)}) copy-start(s32[2]{0:T(128)} %param.7) | copy-start | bytes 28
  1.5 1.9 %collective-permute-start = (bf16[64,16,128]{2,1,0:T(8,128)(2,1)S(1)}, bf16[64,16,128]{2,1,0:T(8,128)(2,1)S(1)}, u32[]{:S(2)}, u32[]{:S(2)}) collective-permute-start(bf16[64,16,128]{2,1,0:T(8,128)(2,1)S(1)} %get-tuple-element.36), channel_id=1, source_target_pairs={{0,64},{64,0},{128,192},{192,128},{1,65},{65,1},{129,193},{193,129... | collective-permute-start | bytes 786440 | tf_op jit(solution)/shard_map/ppermute | solution.py:27
  2.3 3.4 %collective-permute-start.2 = (bf16[16,4,9,264]{3,0,2,1:T(8,128)(2,1)S(1)}, bf16[16,4,9,264]{3,0,2,1:T(8,128)(2,1)S(1)}, u32[]{:S(2)}, u32[]{:S(2)}) collective-permute-start(bf16[16,4,9,264]{3,0,2,1:T(8,128)(2,1)S(1)} %copy.10), channel_id=1, source_target_pairs={{0,64},{64,0},{128,192},{192,128},{1,65},{65,1},{129,193},{193,129... | collective-permute-start | bytes 912392 | tf_op jit(solution)/shard_map/ppermute | solution.py:27
  2.5 35.0 %collective-permute-start.5 = (s32[2,4]{1,0:T(2,128)S(1)}, s32[2,4]{1,0:T(2,128)S(1)}, u32[]{:S(2)}, u32[]{:S(2)}) collective-permute-start(s32[2,4]{1,0:T(2,128)S(1)} %broadcast_multiply_fusion), channel_id=1, source_target_pairs={{0,64},{64,0},{128,192},{192,128},{1,65},{65,1},{129,193},{193,129... | collective-permute-start | bytes 104 | tf_op jit(solution)/shard_map/ppermute | solution.py:27
  3.5 9.1 %collective-permute-start.1 = (bf16[64,16,128]{2,1,0:T(8,128)(2,1)S(1)}, bf16[64,16,128]{2,1,0:T(8,128)(2,1)S(1)}, u32[]{:S(2)}, u32[]{:S(2)}) collective-permute-start(bf16[64,16,128]{2,1,0:T(8,128)(2,1)S(1)} %get-tuple-element.67), channel_id=1, source_target_pairs={{0,128},{64,192},{128,0},{192,64},{1,129},{65,193},{129,1},{193,65... | collective-permute-start | bytes 786440 | tf_op jit(solution)/shard_map/ppermute | solution.py:27
  5.7 22.9 %collective-permute-start.6 = (bf16[64,32,128]{2,1,0:T(8,128)(2,1)S(1)}, bf16[64,32,128]{2,1,0:T(8,128)(2,1)S(1)}, u32[]{:S(2)}, u32[]{:S(2)}) collective-permute-start(bf16[64,32,128]{2,1,0:T(8,128)(2,1)S(1)} %pad_maximum_fusion.refs_0_), channel_id=1, source_target_pairs={{0,1},{1,0},{2,3},{3,2},{4,5},{5,4},{6,7},{7,6},{8,9},{9,8},{10,11... | collective-permute-start | bytes 1572872 | tf_op jit(solution)/shard_map/ppermute | solution.py:33
  12.6 19.5 %collective-permute-start.7 = (bf16[64,32,128]{2,1,0:T(8,128)(2,1)S(1)}, bf16[64,32,128]{2,1,0:T(8,128)(2,1)S(1)}, u32[]{:S(2)}, u32[]{:S(2)}) collective-permute-start(bf16[64,32,128]{2,1,0:T(8,128)(2,1)S(1)} %pad_maximum_fusion.refs_0_), channel_id=1, source_target_pairs={{0,63},{1,2},{2,1},{3,4},{4,3},{5,6},{6,5},{7,8},{8,7},{9,10},{10,... | collective-permute-start | bytes 1572872 | tf_op jit(solution)/shard_map/ppermute | solution.py:33
  21.1 17.3 %collective-permute-start.3 = (bf16[64,16,128]{2,1,0:T(8,128)(2,1)S(1)}, bf16[64,16,128]{2,1,0:T(8,128)(2,1)S(1)}, u32[]{:S(2)}, u32[]{:S(2)}) collective-permute-start(bf16[64,16,128]{2,1,0:T(8,128)(2,1)S(1)} %collective-permute-done.1.refs_3_.refs_5_), channel_id=1, source_target_pairs={{0,1},{1,0},{2,3},{3,2},{4,5},{5,4},{6,7},{7,6},{8,9},{9,8},{10,11... | collective-permute-start | bytes 786440 | tf_op jit(solution)/shard_map/ppermute | solution.py:33
  21.8 16.6 %collective-permute-start.4 = (bf16[64,16,128]{2,1,0:T(8,128)(2,1)S(1)}, bf16[64,16,128]{2,1,0:T(8,128)(2,1)S(1)}, u32[]{:S(2)}, u32[]{:S(2)}) collective-permute-start(bf16[64,16,128]{2,1,0:T(8,128)(2,1)S(1)} %collective-permute-done.1.refs_3_.refs_5_), channel_id=1, source_target_pairs={{0,63},{1,2},{2,1},{3,4},{4,3},{5,6},{6,5},{7,8},{8,7},{9,10},{10,... | collective-permute-start | bytes 786440 | tf_op jit(solution)/shard_map/ppermute | solution.py:33
  32.1 14.9 %collective-permute-start.10 = (bf16[64,32,128]{2,1,0:T(8,128)(2,1)S(1)}, bf16[64,32,128]{2,1,0:T(8,128)(2,1)S(1)}, u32[]{:S(2)}, u32[]{:S(2)}) collective-permute-start(bf16[64,32,128]{2,1,0:T(8,128)(2,1)S(1)} %collective-permute-done.7.refs_2_), channel_id=1, source_target_pairs={{0,1},{1,0},{2,3},{3,2},{4,5},{5,4},{6,7},{7,6},{8,9},{9,8},{10,11... | collective-permute-start | bytes 1572872 | tf_op jit(solution)/shard_map/ppermute | solution.py:33
  32.1 15.0 %collective-permute-start.11 = (bf16[64,32,128]{2,1,0:T(8,128)(2,1)S(1)}, bf16[64,32,128]{2,1,0:T(8,128)(2,1)S(1)}, u32[]{:S(2)}, u32[]{:S(2)}) collective-permute-start(bf16[64,32,128]{2,1,0:T(8,128)(2,1)S(1)} %collective-permute-done.6.refs_1_), channel_id=1, source_target_pairs={{0,63},{1,2},{2,1},{3,4},{4,3},{5,6},{6,5},{7,8},{8,7},{9,10},{10,... | collective-permute-start | bytes 1572872 | tf_op jit(solution)/shard_map/ppermute | solution.py:33
  38.4 13.8 %collective-permute-start.8 = (bf16[64,16,128]{2,1,0:T(8,128)(2,1)S(1)}, bf16[64,16,128]{2,1,0:T(8,128)(2,1)S(1)}, u32[]{:S(2)}, u32[]{:S(2)}) collective-permute-start(bf16[64,16,128]{2,1,0:T(8,128)(2,1)S(1)} %collective-permute-done.4.refs_5_.refs_7_), channel_id=1, source_target_pairs={{0,1},{1,0},{2,3},{3,2},{4,5},{5,4},{6,7},{7,6},{8,9},{9,8},{10,11... | collective-permute-start | bytes 786440 | tf_op jit(solution)/shard_map/ppermute | solution.py:33
  38.5 13.8 %collective-permute-start.9 = (bf16[64,16,128]{2,1,0:T(8,128)(2,1)S(1)}, bf16[64,16,128]{2,1,0:T(8,128)(2,1)S(1)}, u32[]{:S(2)}, u32[]{:S(2)}) collective-permute-start(bf16[64,16,128]{2,1,0:T(8,128)(2,1)S(1)} %collective-permute-done.3.refs_4_.refs_6_), channel_id=1, source_target_pairs={{0,63},{1,2},{2,1},{3,4},{4,3},{5,6},{6,5},{7,8},{8,7},{9,10},{10,... | collective-permute-start | bytes 786440 | tf_op jit(solution)/shard_map/ppermute | solution.py:33
  56.2 7.6 %collective-permute-start.12 = (bf16[16,64,128]{2,1,0:T(8,128)(2,1)S(1)}, bf16[16,64,128]{2,1,0:T(8,128)(2,1)S(1)}, u32[]{:S(2)}, u32[]{:S(2)}) collective-permute-start(bf16[16,64,128]{2,1,0:T(8,128)(2,1)S(1)} %bitcast.22), channel_id=1, source_target_pairs={{0,64},{64,0},{128,192},{192,128},{1,65},{65,1},{129,193},{193,129... | collective-permute-start | bytes 786440 | tf_op jit(solution)/shard_map/ppermute | solution.py:27
where the time goes:
time: 64.9 us; the launch traced here: 64.7 us
  starting transfers between devices  29.9 us (46%)
  Pallas kernels  17.4 us (27%)
  waiting for transfers between devices  12.1 us (19%)
  local copies, waits for them, and re-layouts  2.94 us (5%)
  other arithmetic  2.05 us (3%)
    ppermute x8, starting transfers between devices, pair_swap(): return lax.ppermute(value, 'lon', pairs)  20.2 us
    pallas_call x4, Pallas kernels, conv(): pl.pallas_call(functools.partial(conv_kernel, not done, whiches, counts),...  13.5 us
    ppermute x5, starting transfers between devices, lat_swap(): return lax.ppermute(value, 'lat', [(lat, lat ^ flip) for lat in range(4)])  9.7 us
    ppermute x5, waiting for transfers between devices, lat_swap(): return lax.ppermute(value, 'lat', [(lat, lat ^ flip) for lat in range(4)])  8.37 us
    pallas_call x1, Pallas kernels, left_sides(): pl.pallas_call(prep_kernel, out_shape=[jax.ShapeDtypeStruct((2, K * J * R...  3.9 us
    ppermute x8, waiting for transfers between devices, pair_swap(): return lax.ppermute(value, 'lon', pairs)  3.7 us
    unnamed x9, local copies, waits for them, and re-layouts  1.41 us
  transfers between devices with their start and end apart: 13, of which 5 were waited for; matrix products, arithmetic and copies ran while one was open for 4% of the time, Pallas kernels for 21%

commit v1 on v0

--- a/solution.py
+++ b/solution.py
@@ -36,10 +36,6 @@
 def halo(value):
     near, back = pair_swap(value, 0), pair_swap(value, 1)
     return near, back
-
-
-def beyond(near, back):
-    return pair_swap(back, 0), pair_swap(near, 1)
 
 
 def prep_kernel(place_ref, filt_ref, far_ref, near_ref, spread_ref, pick_ref):
@@ -163,21 +159,33 @@
     out_refs, refs = refs[:some], refs[some:]
     exts, (resp_ref, mixed_ref, sems) = refs[: len(sets)], refs[len(sets) :]
     lon = sets[0][0].shape[0]
-    copies = []
-    for i, pieces in enumerate(sets):
-        copies += fetch(place_ref, pieces, exts[i], sems.at[i])
-    for copy in copies:
-        copy.start()
-    for copy in copies:
-        copy.wait()
+
+    def is_local(group):
+        local = True
+        for b in range(NB):
+            shift = shift_ref[group, b]
+            local = local & (shift >= -lon) & (shift <= lon - BW)
+        return local
+
+    flags = [is_local(2 * which + g) for which in whiches for g in range(2)]
+    flags = flags if early else [jnp.logical_not(flag) for flag in flags]
+
+    @pl.when(functools.reduce(jnp.logical_or, flags))
+    def _():
+        copies = []
+        for i, pieces in enumerate(sets):
+            copies += fetch(place_ref, pieces, exts[i], sems.at[i])
+        for copy in copies:
+            copy.start()
+        for copy in copies:
+            copy.wait()
+
     for n, which in enumerate(whiches):
         left_ref, out_ref = left_refs[n], out_refs[n]
 
         def group(g, carry):
             shifts = [shift_ref[2 * which + g, b] for b in range(NB)]
-            local = True
-            for shift in shifts:
-                local = local & (shift >= -lon) & (shift <= lon - BW)
+            local = is_local(2 * which + g)
 
             @pl.when(local if early else jnp.logical_not(local))
             def _():
@@ -270,15 +278,15 @@
     mix = jnp.where((row_at == col_at)[None], tiled, jnp.zeros_like(tiled))
     mix = mix.reshape(K * chans, chans)
 
-    far_left, near_left, mix, own_near, own_back = together(
-        far_left, near_left, mix, own_near, own_back
-    )
-    own_far_near, own_far_back = beyond(own_near, own_back)
+    own_near, far_left, near_left, mix = together(own_near, far_left, near_left, mix)
+    own_far_back = pair_swap(own_near, 1)
+    own_far_near = pair_swap(own_back, 0)
     own_set, edge_set = [own, own_near, own_back], [edge, edge_near, edge_back]
     (far_done,) = conv([0], place, all_shifts, [own_set], [far_left], mix)
-    edge_near, edge_back, far_done = together(edge_near, edge_back, far_done)
+    edge_far_back = pair_swap(edge_near, 1)
+    edge_back, far_done = together(edge_back, far_done)
+    edge_far_near = pair_swap(edge_back, 0)
     edge_set = [edge, edge_near, edge_back]
-    edge_far_near, edge_far_back = beyond(edge_near, edge_back)
     (near_done,) = conv([1], place, all_shifts, [own_set, edge_set], [near_left], mix)
     own_far_near, own_far_back, near_done = together(own_far_near, own_far_back, near_done)
     own_set = own_set + [own_far_near, own_far_back]

time: 64.9 us -> 63.7 us (0.982)
  the two profiles are of different devices: /device:TPU:17 before, /device:TPU:1 now
where the time goes in v1:
time: 63.7 us; the launch traced here: 63.8 us
  starting transfers between devices  26.5 us (42%)
  Pallas kernels  17.7 us (28%)
  waiting for transfers between devices  14.4 us (23%)
  local copies, waits for them, and re-layouts  2.94 us (5%)
  other arithmetic  2.05 us (3%)
    ppermute x8, starting transfers between devices, pair_swap(): return lax.ppermute(value, 'lon', pairs)  19.4 us
    pallas_call x4, Pallas kernels, conv(): pl.pallas_call(functools.partial(conv_kernel, not done, whiches, counts),...  13.8 us
    ppermute x5, waiting for transfers between devices, lat_swap(): return lax.ppermute(value, 'lat', [(lat, lat ^ flip) for lat in range(4)])  7.35 us
    ppermute x5, starting transfers between devices, lat_swap(): return lax.ppermute(value, 'lat', [(lat, lat ^ flip) for lat in range(4)])  7.11 us
    ppermute x8, waiting for transfers between devices, pair_swap(): return lax.ppermute(value, 'lon', pairs)  7.07 us
    pallas_call x1, Pallas kernels, left_sides(): pl.pallas_call(prep_kernel, out_shape=[jax.ShapeDtypeStruct((2, K * J * R...  3.91 us
    unnamed x9, local copies, waits for them, and re-layouts  1.41 us
  transfers between devices with their start and end apart: 13, of which 5 were waited for; matrix products, arithmetic and copies ran while one was open for 4% of the time, Pallas kernels for 21%

profile of v1, /device:TPU:1, one launch (start us, length us, event | category | flops | bytes accessed | tf_op | source)
XLA Modules:
  0.0 63.8 jit_solution(13427082668539256909)
XLA Ops:
  0.0 1.4 %copy.18 = bf16[16,64,256]{2,0,1:T(8,128)(2,1)S(1)} copy(bf16[16,64,256]{2,1,0:T(8,128)(2,1)} %param.5) | data formatting | bytes 1048576 | tf_op args[0]
  1.5 3.3 %collective-permute-start = (bf16[64,16,128]{2,1,0:T(8,128)(2,1)S(1)}, bf16[64,16,128]{2,1,0:T(8,128)(2,1)S(1)}, u32[]{:S(2)}, u32[]{:S(2)}) collective-permute-start(bf16[64,16,128]{2,1,0:T(8,128)(2,1)S(1)} %get-tuple-element.34), channel_id=1, source_target_pairs={{0,64},{64,0},{128,192},{192,128},{1,65},{65,1},{129,193},{193,129... | collective-permute-start | bytes 786440 | tf_op jit(solution)/shard_map/ppermute | solution.py:27
  5.1 0.5 collective-permute-start.4
  5.6 0.4 collective-permute-done
  6.0 1.3 %collective-permute-start.1 = (bf16[64,16,128]{2,1,0:T(8,128)(2,1)S(1)}, bf16[64,16,128]{2,1,0:T(8,128)(2,1)S(1)}, u32[]{:S(2)}, u32[]{:S(2)}) collective-permute-start(bf16[64,16,128]{2,1,0:T(8,128)(2,1)S(1)} %get-tuple-element.63), channel_id=1, source_target_pairs={{0,128},{64,192},{128,0},{192,64},{1,129},{65,193},{129,1},{193,65... | collective-permute-start | bytes 786440 | tf_op jit(solution)/shard_map/ppermute | solution.py:27
  7.6 1.7 %collective-permute-start.5 = (bf16[64,32,128]{2,1,0:T(8,128)(2,1)S(1)}, bf16[64,32,128]{2,1,0:T(8,128)(2,1)S(1)}, u32[]{:S(2)}, u32[]{:S(2)}) collective-permute-start(bf16[64,32,128]{2,1,0:T(8,128)(2,1)S(1)} %pad_maximum_fusion.refs_0_), channel_id=1, source_target_pairs={{0,1},{1,0},{2,3},{3,2},{4,5},{5,4},{6,7},{7,6},{8,9},{9,8},{10,11... | collective-permute-start | bytes 1572872 | tf_op jit(solution)/shard_map/ppermute | solution.py:33
  9.3 5.8 %collective-permute-done.1.refs_3_.refs_5_ = bf16[64,16,128]{2,1,0:T(8,128)(2,1)S(1)} collective-permute-done((bf16[64,16,128]{2,1,0:T(8,128)(2,1)S(1)}, bf16[64,16,128]{2,1,0:T(8,128)(2,1)S(1)}, u32[]{:S(2)}, u32[]{:S(2)}) %collective-permute-start.1) | collective-permute-done | bytes 262176 | tf_op jit(solution)/shard_map/ppermute | solution.py:27
  15.1 7.1 %collective-permute-start.6 = (bf16[64,32,128]{2,1,0:T(8,128)(2,1)S(1)}, bf16[64,32,128]{2,1,0:T(8,128)(2,1)S(1)}, u32[]{:S(2)}, u32[]{:S(2)}) collective-permute-start(bf16[64,32,128]{2,1,0:T(8,128)(2,1)S(1)} %pad_maximum_fusion.refs_0_), channel_id=1, source_target_pairs={{0,63},{1,2},{2,1},{3,4},{4,3},{5,6},{6,5},{7,8},{8,7},{9,10},{10,... | collective-permute-start | bytes 1572872 | tf_op jit(solution)/shard_map/ppermute | solution.py:33
  22.2 0.3 copy_bitcast_fusion
  22.6 0.4 fusion.2.filt_ref
  23.0 3.9 %shard_map.55 = (bf16[2,144,1152]{2,1,0:T(8,128)(2,1)S(1)}, bf16[2,144,1728]{2,1,0:T(8,128)(2,1)S(1)}) custom-call(s32[3]{0:T(128)S(1)} %pad_add_fusion.1.place_ref, bf16[2,16,4,9,384]{4,3,2,1,0:T(8,128)(2,1)S(1)} %fusion.2.filt_ref), custom_call_target="tpu_custom_call" | custom-call | flops 1 | bytes 1 | tf_op jit(solution)/shard_map/pallas_call | solution.py:88
  27.0 1.1 %tile.4 = bf16[9,8,32,2,128]{4,3,2,1,0:T(2,128)(2,1)S(1)} broadcast(bf16[9,32,128]{2,1,0:T(8,128)(2,1)S(1)} %constant_dynamic-slice_fusion), dimensions={0,2,4} | broadcast | bytes 1253376 | tf_op jit(solution)/shard_map/tile | solution.py:275
  28.1 0.2 bitcast_select_fusion.refs_4_.refs_7_.refs_6_.refs_11_
  28.3 5.7 %collective-permute-start.11 = (bf16[64,32,128]{2,1,0:T(8,128)(2,1)S(1)}, bf16[64,32,128]{2,1,0:T(8,128)(2,1)S(1)}, u32[]{:S(2)}, u32[]{:S(2)}) collective-permute-start(bf16[64,32,128]{2,1,0:T(8,128)(2,1)S(1)} %collective-permute-done.5.refs_1_), channel_id=1, source_target_pairs={{0,63},{1,2},{2,1},{3,4},{4,3},{5,6},{6,5},{7,8},{8,7},{9,10},{10,... | collective-permute-start | bytes 1572872 | tf_op jit(solution)/shard_map/ppermute | solution.py:33
  34.1 4.7 %collective-permute-start.9 = (bf16[64,16,128]{2,1,0:T(8,128)(2,1)S(1)}, bf16[64,16,128]{2,1,0:T(8,128)(2,1)S(1)}, u32[]{:S(2)}, u32[]{:S(2)}) collective-permute-start(bf16[64,16,128]{2,1,0:T(8,128)(2,1)S(1)} %collective-permute-done.8.refs_4_.refs_6_), channel_id=1, source_target_pairs={{0,63},{1,2},{2,1},{3,4},{4,3},{5,6},{6,5},{7,8},{8,7},{9,10},{10,... | collective-permute-start | bytes 786440 | tf_op jit(solution)/shard_map/ppermute | solution.py:33
  38.8 3.0 %shard_map.56.refs_7_ = bf16[2,8,64,128]{3,2,1,0:T(8,128)(2,1)S(1)} custom-call(s32[3]{0:T(128)S(1)} %pad_add_fusion.1.place_ref, s32[4,4]{1,0:T(4,128)S(1)} %pad_add_fusion.shift_ref, bf16[64,32,128]{2,1,0:T(8,128)(2,1)S(1)} %pad_maximum_fusion.refs_0_, bf16[64,32,128]{2,1,0:T(8,128)(2,1)S(1)} %collective-permute-done.5.refs_1_, ...), custom_call_target="tpu_custom_call" | custom-call | flops 1 | bytes 1 | tf_op jit(solution)/shard_map/pallas_call | solution.py:215
  42.0 3.7 %shard_map.57.refs_12_ = bf16[2,8,64,128]{3,2,1,0:T(8,128)(2,1)S(1)} custom-call(s32[3]{0:T(128)S(1)} %pad_add_fusion.1.place_ref, s32[4,4]{1,0:T(4,128)S(1)} %pad_add_fusion.shift_ref, bf16[64,32,128]{2,1,0:T(8,128)(2,1)S(1)} %pad_maximum_fusion.refs_0_, bf16[64,32,128]{2,1,0:T(8,128)(2,1)S(1)} %collective-permute-done.5.refs_1_, ...), custom_call_target="tpu_custom_call" | custom-call | flops 1 | bytes 1 | tf_op jit(solution)/shard_map/pallas_call | solution.py:215
  45.6 4.5 %collective-permute-done.11.refs_4_ = bf16[64,32,128]{2,1,0:T(8,128)(2,1)S(1)} collective-permute-done((bf16[64,32,128]{2,1,0:T(8,128)(2,1)S(1)}, bf16[64,32,128]{2,1,0:T(8,128)(2,1)S(1)}, u32[]{:S(2)}, u32[]{:S(2)}) %collective-permute-start.11) | collective-permute-done | bytes 524320 | tf_op jit(solution)/shard_map/ppermute | solution.py:33
  50.1 3.0 %shard_map.58 = bf16[2,8,64,128]{3,2,1,0:T(8,128)(2,1)S(1)} custom-call(s32[3]{0:T(128)S(1)} %pad_add_fusion.1.place_ref, s32[4,4]{1,0:T(4,128)S(1)} %pad_add_fusion.shift_ref, bf16[64,32,128]{2,1,0:T(8,128)(2,1)S(1)} %pad_maximum_fusion.refs_0_, bf16[64,32,128]{2,1,0:T(8,128)(2,1)S(1)} %collective-permute-done.5.refs_1_, ...), custom_call_target="tpu_custom_call" | custom-call | flops 1 | bytes 1 | tf_op jit(solution)/shard_map/pallas_call | solution.py:215
  53.1 2.6 %collective-permute-done.9.refs_9_ = bf16[64,16,128]{2,1,0:T(8,128)(2,1)S(1)} collective-permute-done((bf16[64,16,128]{2,1,0:T(8,128)(2,1)S(1)}, bf16[64,16,128]{2,1,0:T(8,128)(2,1)S(1)}, u32[]{:S(2)}, u32[]{:S(2)}) %collective-permute-start.9) | collective-permute-done | bytes 262176 | tf_op jit(solution)/shard_map/ppermute | solution.py:33
  55.7 4.1 %shard_map.59 = bf16[2,8,64,128]{3,2,1,0:T(8,128)(2,1)S(1)} custom-call(s32[3]{0:T(128)S(1)} %pad_add_fusion.1.place_ref, s32[4,4]{1,0:T(4,128)S(1)} %pad_add_fusion.shift_ref, bf16[64,32,128]{2,1,0:T(8,128)(2,1)S(1)} %pad_maximum_fusion.refs_0_, bf16[64,32,128]{2,1,0:T(8,128)(2,1)S(1)} %collective-permute-done.5.refs_1_, ...), custom_call_target="tpu_custom_call" | custom-call | flops 1 | bytes 1 | tf_op jit(solution)/shard_map/pallas_call | solution.py:215
  59.9 1.9 %collective-permute-start.12 = (bf16[16,64,128]{2,1,0:T(8,128)(2,1)S(1)}, bf16[16,64,128]{2,1,0:T(8,128)(2,1)S(1)}, u32[]{:S(2)}, u32[]{:S(2)}) collective-permute-start(bf16[16,64,128]{2,1,0:T(8,128)(2,1)S(1)} %bitcast.22), channel_id=1, source_target_pairs={{0,64},{64,0},{128,192},{192,128},{1,65},{65,1},{129,193},{193,129... | collective-permute-start | bytes 786440 | tf_op jit(solution)/shard_map/ppermute | solution.py:27
  61.8 1.2 %collective-permute-done.12 = bf16[16,64,128]{2,1,0:T(8,128)(2,1)S(1)} collective-permute-done((bf16[16,64,128]{2,1,0:T(8,128)(2,1)S(1)}, bf16[16,64,128]{2,1,0:T(8,128)(2,1)S(1)}, u32[]{:S(2)}, u32[]{:S(2)}) %collective-permute-start.12) | collective-permute-done | bytes 262176 | tf_op jit(solution)/shard_map/ppermute | solution.py:27
  63.0 0.9 %pad_maximum_fusion.1 = bf16[16,64,256]{2,1,0:T(8,128)(2,1)} fusion(bf16[16,64,128]{2,1,0:T(8,128)(2,1)S(1)} %get-tuple-element.67, bf16[16,64,128]{2,1,0:T(8,128)(2,1)S(1)} %get-tuple-element.66), kind=kLoop, calls=%fused_computation.8 | loop fusion | flops 1048576 | bytes 1048576 | tf_op jit(solution)/shard_map/concatenate | solution.py:302
  (36 shorter events, 1.1 us)
Async XLA Ops:
  0.0 26.9 %copy-start = (bf16[9,32,256]{2,1,0:T(8,128)(2,1)S(1)}, bf16[9,32,256]{2,1,0:T(8,128)(2,1)}, u32[]{:S(2)}) copy-start(bf16[9,32,256]{2,1,0:T(8,128)(2,1)} %param.9) | copy-start | bytes 442372
  0.0 4.8 %copy-start.1 = (bf16[16,4,9,264]{3,1,2,0:T(4,128)(2,1)S(1)}, bf16[16,4,9,264]{3,1,2,0:T(4,128)(2,1)}, u32[]{:S(2)}) copy-start(bf16[16,4,9,264]{3,1,2,0:T(4,128)(2,1)} %param.6) | copy-start | bytes 912388
  0.0 5.0 %copy-start.2 = (s32[2,4]{1,0:T(2,128)S(1)}, s32[2,4]{1,0:T(2,128)}, u32[]{:S(2)}) copy-start(s32[2,4]{1,0:T(2,128)} %param.8) | copy-start | bytes 100
  0.0 5.0 %copy-start.3 = (s32[2]{0:T(128)S(1)}, s32[2]{0:T(128)}, u32[]{:S(2)}) copy-start(s32[2]{0:T(128)} %param.7) | copy-start | bytes 28
  1.5 4.5 %collective-permute-start = (bf16[64,16,128]{2,1,0:T(8,128)(2,1)S(1)}, bf16[64,16,128]{2,1,0:T(8,128)(2,1)S(1)}, u32[]{:S(2)}, u32[]{:S(2)}) collective-permute-start(bf16[64,16,128]{2,1,0:T(8,128)(2,1)S(1)} %get-tuple-element.34), channel_id=1, source_target_pairs={{0,64},{64,0},{128,192},{192,128},{1,65},{65,1},{129,193},{193,129... | collective-permute-start | bytes 786440 | tf_op jit(solution)/shard_map/ppermute | solution.py:27
  4.9 4.5 %collective-permute-start.2 = (bf16[16,4,9,264]{3,0,2,1:T(8,128)(2,1)S(1)}, bf16[16,4,9,264]{3,0,2,1:T(8,128)(2,1)S(1)}, u32[]{:S(2)}, u32[]{:S(2)}) collective-permute-start(bf16[16,4,9,264]{3,0,2,1:T(8,128)(2,1)S(1)} %copy.10), channel_id=1, source_target_pairs={{0,64},{64,0},{128,192},{192,128},{1,65},{65,1},{129,193},{193,129... | collective-permute-start | bytes 912392 | tf_op jit(solution)/shard_map/ppermute | solution.py:27
  5.1 29.0 %collective-permute-start.4 = (s32[2,4]{1,0:T(2,128)S(1)}, s32[2,4]{1,0:T(2,128)S(1)}, u32[]{:S(2)}, u32[]{:S(2)}) collective-permute-start(s32[2,4]{1,0:T(2,128)S(1)} %broadcast_multiply_fusion), channel_id=1, source_target_pairs={{0,64},{64,0},{128,192},{192,128},{1,65},{65,1},{129,193},{193,129... | collective-permute-start | bytes 104 | tf_op jit(solution)/shard_map/ppermute | solution.py:27
  6.0 9.1 %collective-permute-start.1 = (bf16[64,16,128]{2,1,0:T(8,128)(2,1)S(1)}, bf16[64,16,128]{2,1,0:T(8,128)(2,1)S(1)}, u32[]{:S(2)}, u32[]{:S(2)}) collective-permute-start(bf16[64,16,128]{2,1,0:T(8,128)(2,1)S(1)} %get-tuple-element.63), channel_id=1, source_target_pairs={{0,128},{64,192},{128,0},{192,64},{1,129},{65,193},{129,1},{193,65... | collective-permute-start | bytes 786440 | tf_op jit(solution)/shard_map/ppermute | solution.py:27
  7.6 20.7 %collective-permute-start.5 = (bf16[64,32,128]{2,1,0:T(8,128)(2,1)S(1)}, bf16[64,32,128]{2,1,0:T(8,128)(2,1)S(1)}, u32[]{:S(2)}, u32[]{:S(2)}) collective-permute-start(bf16[64,32,128]{2,1,0:T(8,128)(2,1)S(1)} %pad_maximum_fusion.refs_0_), channel_id=1, source_target_pairs={{0,1},{1,0},{2,3},{3,2},{4,5},{5,4},{6,7},{7,6},{8,9},{9,8},{10,11... | collective-permute-start | bytes 1572872 | tf_op jit(solution)/shard_map/ppermute | solution.py:33
  15.1 18.9 %collective-permute-start.6 = (bf16[64,32,128]{2,1,0:T(8,128)(2,1)S(1)}, bf16[64,32,128]{2,1,0:T(8,128)(2,1)S(1)}, u32[]{:S(2)}, u32[]{:S(2)}) collective-permute-start(bf16[64,32,128]{2,1,0:T(8,128)(2,1)S(1)} %pad_maximum_fusion.refs_0_), channel_id=1, source_target_pairs={{0,63},{1,2},{2,1},{3,4},{4,3},{5,6},{6,5},{7,8},{8,7},{9,10},{10,... | collective-permute-start | bytes 1572872 | tf_op jit(solution)/shard_map/ppermute | solution.py:33
  22.2 19.7 %collective-permute-start.3 = (bf16[64,16,128]{2,1,0:T(8,128)(2,1)S(1)}, bf16[64,16,128]{2,1,0:T(8,128)(2,1)S(1)}, u32[]{:S(2)}, u32[]{:S(2)}) collective-permute-start(bf16[64,16,128]{2,1,0:T(8,128)(2,1)S(1)} %collective-permute-done.1.refs_3_.refs_5_), channel_id=1, source_target_pairs={{0,63},{1,2},{2,1},{3,4},{4,3},{5,6},{6,5},{7,8},{8,7},{9,10},{10,... | collective-permute-start | bytes 786440 | tf_op jit(solution)/shard_map/ppermute | solution.py:33
  22.9 11.2 %collective-permute-start.8 = (bf16[64,16,128]{2,1,0:T(8,128)(2,1)S(1)}, bf16[64,16,128]{2,1,0:T(8,128)(2,1)S(1)}, u32[]{:S(2)}, u32[]{:S(2)}) collective-permute-start(bf16[64,16,128]{2,1,0:T(8,128)(2,1)S(1)} %collective-permute-done.1.refs_3_.refs_5_), channel_id=1, source_target_pairs={{0,1},{1,0},{2,3},{3,2},{4,5},{5,4},{6,7},{7,6},{8,9},{9,8},{10,11... | collective-permute-start | bytes 786440 | tf_op jit(solution)/shard_map/ppermute | solution.py:33
  28.3 21.8 %collective-permute-start.11 = (bf16[64,32,128]{2,1,0:T(8,128)(2,1)S(1)}, bf16[64,32,128]{2,1,0:T(8,128)(2,1)S(1)}, u32[]{:S(2)}, u32[]{:S(2)}) collective-permute-start(bf16[64,32,128]{2,1,0:T(8,128)(2,1)S(1)} %collective-permute-done.5.refs_1_), channel_id=1, source_target_pairs={{0,63},{1,2},{2,1},{3,4},{4,3},{5,6},{6,5},{7,8},{8,7},{9,10},{10,... | collective-permute-start | bytes 1572872 | tf_op jit(solution)/shard_map/ppermute | solution.py:33
  34.1 16.0 %collective-permute-start.10 = (bf16[64,32,128]{2,1,0:T(8,128)(2,1)S(1)}, bf16[64,32,128]{2,1,0:T(8,128)(2,1)S(1)}, u32[]{:S(2)}, u32[]{:S(2)}) collective-permute-start(bf16[64,32,128]{2,1,0:T(8,128)(2,1)S(1)} %collective-permute-done.6.refs_2_), channel_id=1, source_target_pairs={{0,1},{1,0},{2,3},{3,2},{4,5},{5,4},{6,7},{7,6},{8,9},{9,8},{10,11... | collective-permute-start | bytes 1572872 | tf_op jit(solution)/shard_map/ppermute | solution.py:33
  34.1 21.6 %collective-permute-start.9 = (bf16[64,16,128]{2,1,0:T(8,128)(2,1)S(1)}, bf16[64,16,128]{2,1,0:T(8,128)(2,1)S(1)}, u32[]{:S(2)}, u32[]{:S(2)}) collective-permute-start(bf16[64,16,128]{2,1,0:T(8,128)(2,1)S(1)} %collective-permute-done.8.refs_4_.refs_6_), channel_id=1, source_target_pairs={{0,63},{1,2},{2,1},{3,4},{4,3},{5,6},{6,5},{7,8},{8,7},{9,10},{10,... | collective-permute-start | bytes 786440 | tf_op jit(solution)/shard_map/ppermute | solution.py:33
  41.9 13.9 %collective-permute-start.7 = (bf16[64,16,128]{2,1,0:T(8,128)(2,1)S(1)}, bf16[64,16,128]{2,1,0:T(8,128)(2,1)S(1)}, u32[]{:S(2)}, u32[]{:S(2)}) collective-permute-start(bf16[64,16,128]{2,1,0:T(8,128)(2,1)S(1)} %collective-permute-done.3.refs_5_.refs_7_), channel_id=1, source_target_pairs={{0,1},{1,0},{2,3},{3,2},{4,5},{5,4},{6,7},{7,6},{8,9},{9,8},{10,11... | collective-permute-start | bytes 786440 | tf_op jit(solution)/shard_map/ppermute | solution.py:33
  59.9 3.1 %collective-permute-start.12 = (bf16[16,64,128]{2,1,0:T(8,128)(2,1)S(1)}, bf16[16,64,128]{2,1,0:T(8,128)(2,1)S(1)}, u32[]{:S(2)}, u32[]{:S(2)}) collective-permute-start(bf16[16,64,128]{2,1,0:T(8,128)(2,1)S(1)} %bitcast.22), channel_id=1, source_target_pairs={{0,64},{64,0},{128,192},{192,128},{1,65},{65,1},{129,193},{193,129... | collective-permute-start | bytes 786440 | tf_op jit(solution)/shard_map/ppermute | solution.py:27
